TPU v7x, 128 devices: a whole 4x4x4 slice. The times are simulated.
128 devices in a mesh: ctx: 16 (over y, z), chan: 8 (over x, core).
Axes of the slice: x: 4, y: 4, z: 4, core: 2. Of those that a mesh axis runs over, the one named last changes fastest.
Arguments:
- signal: bfloat16 [8, 524288], P(None, ('ctx', 'chan')), may hold values from -0.015625 to 0.015625
- grad_out: bfloat16 [8, 524288], P(None, ('ctx', 'chan')), may hold values from -6 to 6
- residue: float32 [8, 16], P('chan'), may hold values from -2 to 2
- decay_rate: float32 [8, 16], P('chan'), may hold values from 1.9073486e-06 to 0.06
Outputs:
- grad_signal: bfloat16 [8, 524288], P(None, ('ctx', 'chan'))
- residue_grad: float32 [8, 16], P('chan')
- lograte_grad: float32 [8, 16], P('chan')
All inputs are finite; a program needn't handle non-finite values.
Results may differ from a plain program's by a relative error of at most 0.013.
Values may be sent and summed in bfloat16 or wider, within the bound.
A program may use at most 192 MiB of HBM per device.

v0:
```python
import math

import jax
import jax.numpy as jnp
from jax import lax
from jax.sharding import PartitionSpec as P

RADIX = 256


highest = lax.Precision.HIGHEST


def shortened(array):

    def short(part):
        return part.astype(jnp.bfloat16) if part.dtype == jnp.float32 else part

    return jax.tree.map(short, array)


def unit_roots(products, modulus):
    angles = (products % modulus).astype(jnp.float32) * (2.0 * math.pi / modulus)
    return (jnp.cos(angles), jnp.sin(angles))


def roots_table(row_count, col_count, modulus):
    row_ids = jnp.arange(row_count, dtype=jnp.int32)[:, None]
    col_ids = jnp.arange(col_count, dtype=jnp.int32)[None, :]
    return unit_roots(row_ids * col_ids, modulus)


def rotate(stacked, cosines, sines, direction):
    real_part = stacked[0] * cosines + direction * stacked[1] * sines
    imag_part = stacked[1] * cosines - direction * stacked[0] * sines
    return jnp.stack([real_part, imag_part])


def dft_section(stacked, cosines, sines, pattern, direction):
    with_cos = jnp.einsum(pattern, stacked, cosines, precision=highest)
    with_sin = jnp.einsum(pattern, stacked, sines, precision=highest)
    real_part = with_cos[0] + direction * with_sin[1]
    imag_part = with_cos[1] - direction * with_sin[0]
    return jnp.stack([real_part, imag_part])


def forward_local(stacked, outer_len, seq_block):
    shaped = stacked.reshape(stacked.shape[:-1] + (outer_len, RADIX))
    outer_cos, outer_sin = roots_table(outer_len, outer_len, outer_len)
    shaped = dft_section(shaped, outer_cos, outer_sin, "zsheab,ac->zshecb", 1.0)
    twist_cos, twist_sin = roots_table(outer_len, RADIX, seq_block)
    shaped = rotate(shaped, twist_cos, twist_sin, 1.0)
    inner_cos, inner_sin = roots_table(RADIX, RADIX, RADIX)
    return dft_section(shaped, inner_cos, inner_sin, "zshecb,bd->zshecd", 1.0)


def inverse_local(stacked, outer_len, seq_block):
    inner_cos, inner_sin = roots_table(RADIX, RADIX, RADIX)
    shaped = dft_section(stacked, inner_cos, inner_sin, "zshecd,db->zshecb", -1.0)
    twist_cos, twist_sin = roots_table(outer_len, RADIX, seq_block)
    shaped = rotate(shaped, twist_cos, twist_sin, -1.0)
    outer_cos, outer_sin = roots_table(outer_len, outer_len, outer_len)
    shaped = dft_section(shaped, outer_cos, outer_sin, "zshecb,ca->zsheab", -1.0)
    return shaped.reshape(shaped.shape[:-2] + (seq_block,))


def decay_rows(decay_rate, positions):
    return jnp.exp(-decay_rate[:, :, None] * positions[None, None, :])


def time_sums(filter_grad, residue, decay_rate, root_rate, positions):
    decays = decay_rows(decay_rate, positions)
    plain_sum = jnp.einsum("hkb,hb->hk", decays, filter_grad, precision=highest)
    tilted_rows = decays * (0.5 - decay_rate[:, :, None] * positions[None, None, :])
    tilted = jnp.einsum("hkb,hb->hk", tilted_rows, filter_grad, precision=highest)
    return (root_rate * plain_sum, residue * root_rate * tilted)


def on_device(signal, grad_out, residue, decay_rate):
    both_inputs = jnp.stack([signal, grad_out])
    laid_out = lax.all_to_all(both_inputs, "chan", split_axis=1, concat_axis=2, tiled=True)
    chan_rows = laid_out.shape[1]
    seq_block = laid_out.shape[2]
    ctx_count = lax.axis_size("ctx")
    sub_block = seq_block // ctx_count
    fft_len = 2 * ctx_count * seq_block
    outer_len = seq_block // RADIX
    ctx_index = lax.axis_index("ctx")
    root_rate = jnp.sqrt(decay_rate)
    own_positions = (ctx_index * seq_block + jnp.arange(seq_block, dtype=jnp.int32)).astype(
        jnp.float32
    )
    spread_inputs = lax.all_to_all(
        laid_out.reshape(2, chan_rows, 1, seq_block), "ctx", split_axis=3, concat_axis=2, tiled=True
    )
    columns_in = spread_inputs.astype(jnp.float32)
    filter_rows = jnp.einsum(
        "hk,hkb->hb", residue * root_rate, decay_rows(decay_rate, own_positions), precision=highest
    )
    spread_filter = lax.all_to_all(
        filter_rows.reshape(chan_rows, 1, seq_block).astype(jnp.bfloat16),
        "ctx",
        split_axis=2,
        concat_axis=1,
        tiled=True,
    ).astype(jnp.float32)
    columns_in = jnp.concatenate([columns_in, spread_filter[None]], axis=0)
    class_order = jnp.arange(2 * ctx_count, dtype=jnp.int32)
    piece_ids = jnp.arange(ctx_count, dtype=jnp.int32)
    piece_cos, piece_sin = unit_roots(piece_ids[:, None] * class_order[None, :], 2 * ctx_count)
    real_cols = jnp.einsum("shpj,pk->shkj", columns_in, piece_cos, precision=highest)
    imag_cols = -jnp.einsum("shpj,pk->shkj", columns_in, piece_sin, precision=highest)
    local_cols = ctx_index * sub_block + jnp.arange(sub_block, dtype=jnp.int32)
    wave_cos, wave_sin = unit_roots(class_order[:, None] * local_cols[None, :], fft_len)
    spectra_cols = rotate(jnp.stack([real_cols, imag_cols]), wave_cos, wave_sin, 1.0)
    gathered = lax.all_to_all(spectra_cols, "ctx", split_axis=3, concat_axis=4, tiled=True)
    spectra = forward_local(gathered, outer_len, seq_block)
    pair_freq = lax.dynamic_slice_in_dim(class_order, 2 * ctx_index, 2)
    signal_re, signal_im = (spectra[0, 0], spectra[1, 0])
    grad_re, grad_im = (spectra[0, 1], spectra[1, 1])
    filter_re, filter_im = (spectra[0, 2], spectra[1, 2])
    back_re = filter_re * grad_re + filter_im * grad_im
    back_im = filter_re * grad_im - filter_im * grad_re
    corr_re = grad_re * signal_re + grad_im * signal_im
    corr_im = grad_im * signal_re - grad_re * signal_im
    products = jnp.stack([jnp.stack([back_re, corr_re]), jnp.stack([back_im, corr_im])])
    inverse_rows = inverse_local(products, outer_len, seq_block)
    all_columns = jnp.arange(seq_block, dtype=jnp.int32)
    turn_cos, turn_sin = unit_roots(pair_freq[:, None] * all_columns[None, :], fft_len)
    inverse_rows = rotate(inverse_rows, turn_cos, turn_sin, -1.0)
    regathered = lax.all_to_all(
        shortened(inverse_rows), "ctx", split_axis=4, concat_axis=3, tiled=True
    ).astype(inverse_rows.dtype)
    back_cos, back_sin = unit_roots(class_order[:, None] * piece_ids[None, :], 2 * ctx_count)
    real_rows = (
        jnp.einsum("shkj,kp->shpj", regathered[0], back_cos, precision=highest)
        - jnp.einsum("shkj,kp->shpj", regathered[1], back_sin, precision=highest)
    ) * (1.0 / fft_len)
    returned = lax.all_to_all(real_rows, "ctx", split_axis=2, concat_axis=3, tiled=True)
    grad_rows = returned[0, :, 0, :].astype(jnp.bfloat16)
    residue_part, lograte_part = time_sums(
        returned[1, :, 0, :], residue, decay_rate, root_rate, own_positions
    )
    residue_grad, lograte_grad = lax.psum((residue_part, lograte_part), "ctx")
    grad_signal = lax.all_to_all(grad_rows, "chan", split_axis=1, concat_axis=0, tiled=True)
    return (grad_signal, residue_grad, lograte_grad)


def solution(mesh):
    return jax.shard_map(
        on_device,
        mesh=mesh,
        in_specs=(
            P(None, ("ctx", "chan")),
            P(None, ("ctx", "chan")),
            P("chan", None),
            P("chan", None),
        ),
        out_specs=(P(None, ("ctx", "chan")), P("chan", None), P("chan", None)),
        check_vma=False,
    )
```

profile of v0, /device:TPU:1, one launch (start us, length us, event | category | flops | bytes accessed | tf_op | source)
XLA Modules:
  0.0 1326.8 jit_solution(17099213636480646017)
XLA Ops:
  1.3 5.4 subtract_multiply_fusion
  6.7 2.2 fusion.8
  9.0 110.0 %reshape_bitcast_fusion = bf16[32768,1,1]{2,1,0:T(2,128)(2,1)} fusion(bf16[32768]{0:T(1024)(128)(2,1)S(1)} %convert_element_type.141), kind=kLoop, calls=%fused_computation.226 | loop fusion | bytes 131072
  119.5 245.4 %reduce.2 = bf16[32768]{0:T(1024)(128)(2,1)S(1)} reduce(bf16[32768,1,1]{2,1,0:T(2,128)(2,1)} %reshape_bitcast_fusion, bf16[]{:T(256)} %broadcast.782), dimensions={1,2}, to_apply=%reshape_bitcast_fusion.reduce_sub_computation | reduce | bytes 131074
  365.6 8.6 all-to-all-start.2
  374.2 0.8 copy.92
  375.0 5.7 all-to-all-done.2
  380.7 7.0 all-to-all-start
  387.6 1.0 fusion.69
  388.8 19.3 %reshape.1149 = bf16[32768,1,1]{2,1,0:T(2,128)(2,1)} reshape(bf16[16,2,1024]{2,1,0:T(2,128)(2,1)S(1)} %all-to-all-done.2) | data formatting | bytes 131072
  408.1 25.3 %copy.93 = bf16[2,1,1,32768]{0,2,1,3:T(2,128)(2,1)} copy(bf16[2,1,1,32768]{3,0,2,1:T(2,128)(2,1)S(1)} %bitcast.237) | data formatting | bytes 262144 | tf_op jit(solution)/shard_map/reshape | solution.py:94
  433.5 179.1 %reduce.3 = bf16[32768,2]{1,0:T(8,128)(2,1)} reduce(bf16[32768,1,1,2]{3,2,1,0:T(2,128)(2,1)} %bitcast.227, bf16[]{:T(256)} %broadcast.782), dimensions={1,2}, to_apply=%bitcast.202.reduce_sub_computation | reduce | bytes 262146
  612.6 13.7 %reshape.1150 = bf16[16,2,2048]{2,1,0:T(2,128)(2,1)} reshape(bf16[32768,2]{1,0:T(8,128)(2,1)} %reduce.3) | data formatting | bytes 262144
  626.3 3.7 all-to-all-start.1
  630.0 244.8 %bitcast_reduce_fusion = bf16[32768]{0:T(1024)(128)(2,1)S(1)} fusion(bf16[32768,1,1]{2,1,0:T(2,128)(2,1)} %reshape.1149), kind=kLoop, calls=%fused_computation.225 | loop fusion | bytes 131072 | tf_op jit(solution)/shard_map/all_to_all | solution.py:100
  874.8 20.8 %reshape.1151 = bf16[32768,1,1,2]{3,2,1,0:T(2,128)(2,1)} reshape(bf16[16,2,2048]{2,1,0:T(2,128)(2,1)S(1)} %all-to-all-done.1) | data formatting | bytes 262144
  895.6 30.6 %copy.94 = bf16[2,1,1,32768]{3,0,2,1:T(2,128)(2,1)S(1)} copy(bf16[2,1,1,32768]{0,2,1,3:T(2,128)(2,1)} %bitcast.228) | data formatting | bytes 262144 | tf_op jit(solution)/shard_map/all_to_all | solution.py:93
  926.8 0.7 add_bitcast_fusion
  927.6 2.4 copy.97
  930.0 6.7 all-to-all-start.3
  936.7 5.1 fusion.59
  942.9 16.7 %all-to-all-done.3 = f32[2,3,1,32,2048]{4,0,2,1,3:T(2,128)} async-done(((f32[2,3,1,32,2048]{4,0,2,1,3:T(2,128)}), f32[2,3,1,32,2048]{4,0,2,1,3:T(2,128)}, u32[]{:S(2)}, u32[]{:S(2)}) %all-to-all-start.3) | async-done | bytes 1572896 | tf_op jit(solution)/shard_map/all_to_all | solution.py:116
  959.5 3.5 copy.136
  963.0 2.7 reshape.1126
  965.8 3.2 convolution_bitcast_fusion.1
  969.0 1.7 convolution_bitcast_fusion.2
  971.0 2.4 fusion.12
  973.4 2.4 fusion.13
  976.4 2.0 fusion.20
  978.4 2.4 fusion.21
  980.9 1.3 convolution_bitcast_fusion.3
  982.2 1.3 convolution_bitcast_fusion.4
  983.5 0.9 fusion.23
  984.8 1.4 add.303
  986.2 1.5 fusion.50
  987.7 0.7 pad_maximum_fusion.1
  988.4 52.8 %copy.105 = bf16[2,2,1,2,32768]{3,1,2,0,4:T(2,128)(2,1)} copy(bf16[2,2,1,2,32768]{4,3,1,2,0:T(2,128)(2,1)S(1)} %pad_maximum_fusion.1) | data formatting | bytes 1048576 | tf_op jit(solution)/shard_map/stack | solution.py:36
  1041.2 61.2 %reshape.1152 = bf16[16,2,8192]{2,1,0:T(2,128)(2,1)S(1)} reshape(bf16[32768,2,1,2,2]{4,3,2,1,0:T(2,128)(2,1)} %bitcast.225) | data formatting | bytes 1048576
  1102.4 12.8 all_to_all.79
  1115.2 73.4 %reshape.1153 = bf16[32768,2,1,2,2]{4,3,2,1,0:T(2,128)(2,1)} reshape(bf16[16,2,8192]{2,1,0:T(2,128)(2,1)S(1)} %all_to_all.79) | data formatting | bytes 1048576
  1188.5 76.4 %copy.106 = bf16[2,2,1,2,16,2048]{5,3,4,1,2,0:T(2,128)(2,1)S(1)} copy(bf16[2,2,1,2,16,2048]{3,1,0,5,4,2:T(2,128)(2,1)} %bitcast.226) | data formatting | bytes 1048576 | tf_op jit(solution)/shard_map/all_to_all | solution.py:131
  1266.4 10.4 all_to_all.80
  1276.8 1.0 reduce.4
  1278.5 8.9 all-to-all-start.6
  1287.6 4.9 fusion.17
  1292.5 3.3 fusion.14
  1295.8 30.1 %all-reduce = (f32[1,16]{1,0:T(1,128)}, f32[1,16]{1,0:T(1,128)}) all-reduce(f32[1,16]{1,0:T(1,128)S(1)} %fusion.14, f32[1,16]{1,0:T(1,128)S(1)} %fusion.17), channel_id=1, replica_groups=mesh['ctx'=16,'chan'=8] {'ctx'}, use_global_device_ids=true, to_apply=%region_0.1 | all-reduce | flops 32 | bytes 256 | tf_op jit(solution)/shard_map/psum | solution.py:144
  1325.9 0.7 copy.138
  (46 shorter events, 7.4 us)
Async XLA Ops:
  1.3 5.4 copy-start.3
  1.3 5.4 copy-start.4
  119.5 254.7 %copy-start.1 = (bf16[8,4096]{1,0:T(8,128)(2,1)S(1)}, bf16[8,4096]{1,0:T(8,128)(2,1)}, u32[]{:S(2)}) copy-start(bf16[8,4096]{1,0:T(8,128)(2,1)} %param.5) | copy-start | bytes 196612
  119.5 254.7 %copy-start.2 = (bf16[8,4096]{1,0:T(8,128)(2,1)S(1)}, bf16[8,4096]{1,0:T(8,128)(2,1)}, u32[]{:S(2)}) copy-start(bf16[8,4096]{1,0:T(8,128)(2,1)} %param.4) | copy-start | bytes 196612
  365.6 15.1 %all-to-all-start.2 = ((bf16[16,2,1024]{2,1,0:T(2,128)(2,1)}), bf16[16,2,1024]{2,1,0:T(2,128)(2,1)S(1)}, u32[]{:S(2)}, u32[]{:S(2)}) async-start(bf16[16,2,1024]{2,1,0:T(2,128)(2,1)} %reshape.1148), calls=%async_computation.2 | async-start | bytes 131072 | tf_op jit(solution)/shard_map/all_to_all | solution.py:100
  380.7 27.4 %all-to-all-start = ((bf16[2,8,4096]{2,0,1:T(2,128)(2,1)}), bf16[2,8,4096]{2,0,1:T(2,128)(2,1)S(1)}, u32[]{:S(2)}, u32[]{:S(2)}) async-start(bf16[2,8,4096]{2,0,1:T(2,128)(2,1)} %copy.92), calls=%async_computation | async-start | bytes 262144 | tf_op jit(solution)/shard_map/all_to_all | solution.py:81
  626.3 248.5 %all-to-all-start.1 = ((bf16[16,2,2048]{2,1,0:T(2,128)(2,1)}), bf16[16,2,2048]{2,1,0:T(2,128)(2,1)S(1)}, u32[]{:S(2)}, u32[]{:S(2)}) async-start(bf16[16,2,2048]{2,1,0:T(2,128)(2,1)} %reshape.1150), calls=%async_computation.1 | async-start | bytes 262144 | tf_op jit(solution)/shard_map/all_to_all | solution.py:93
  930.0 29.6 %all-to-all-start.3 = ((f32[2,3,1,32,2048]{4,0,2,1,3:T(2,128)}), f32[2,3,1,32,2048]{4,0,2,1,3:T(2,128)}, u32[]{:S(2)}, u32[]{:S(2)}) async-start(f32[2,3,1,32,2048]{4,0,2,1,3:T(2,128)} %copy.97), calls=%async_computation.3 | async-start | bytes 3145728 | tf_op jit(solution)/shard_map/all_to_all | solution.py:116
  965.7 3.2 copy-start
  1278.5 47.4 %all-to-all-start.6 = ((bf16[8,2,2048]{2,1,0:T(2,128)(2,1)}), bf16[8,2,2048]{2,1,0:T(2,128)(2,1)S(1)}, u32[]{:S(2)}, u32[]{:S(2)}) async-start(bf16[8,2,2048]{2,1,0:T(2,128)(2,1)} %reshape.1154), calls=%async_computation.6 | async-start | bytes 131072 | tf_op jit(solution)/shard_map/all_to_all | solution.py:145
where the time goes:
time: 1340 us; the launch traced here: 1330 us
  local copies, waits for them, and re-layouts  743 us (55%)
  other arithmetic  443 us (33%)
  blocking collectives  53.2 us (4%)
  starting transfers between devices  34.9 us (3%)
  matrix products  29 us (2%)
  waiting for transfers between devices  22.3 us (2%)
    unnamed x3, other arithmetic  426 us
    unnamed x22, local copies, waits for them, and re-layouts  301 us
    all_to_all x1, local copies, waits for them, and re-layouts, on_device(): lax.all_to_all(filter_rows.reshape(chan_rows, 1, seq_block).astype(jnp.bf...  245 us
    all_to_all x1, local copies, waits for them, and re-layouts, on_device(): lax.all_to_all(shortened(inverse_rows), 'ctx', split_axis=4, concat_axis=...  76.4 us
    another operation x2, local copies, waits for them, and re-layouts, rotate(): return jnp.stack([real_part, imag_part])  55.1 us
    all_to_all x1, local copies, waits for them, and re-layouts, on_device(): lax.all_to_all(laid_out.reshape(2, chan_rows, 1, seq_block), 'ctx', split...  30.6 us
    psum x1, blocking collectives, on_device(): residue_grad, lograte_grad = lax.psum((residue_part, lograte_part), 'ctx')  30.1 us
  transfers between devices with their start and end apart: 5, of which 2 were waited for; matrix products, arithmetic and copies ran while one was open for 21% of the time, Pallas kernels for 0%

commit v1 on v0

v1 whole, which is shorter than its diff:
```python
import functools

import jax
import jax.numpy as jnp
from jax import lax
from jax.experimental import pallas as pl
from jax.experimental.pallas import tpu as pltpu
from jax.sharding import PartitionSpec as P

MESH = pl.DeviceIdType.MESH
LANES = 128
F32 = jnp.float32
BF16 = jnp.bfloat16


def split(value):
    high = value.astype(BF16)
    return high, (value - high.astype(F32)).astype(BF16)


def iota(shape, axis):
    return lax.broadcasted_iota(jnp.int32, shape, axis)


def lift(array, step):
    rows = array.shape[0]
    moved = pltpu.roll(array, rows - step, axis=0)
    return jnp.where(iota(array.shape, 0) < rows - step, moved, 0.0)


def scan(e, ed, rate, length):
    rows = e.shape[0]
    step = 1
    while step < rows:
        fade = jnp.exp(-rate * float(step * length))
        up, upd = lift(e, step), lift(ed, step)
        e, ed = e + fade * up, ed + fade * (upd + float(step * length) * up)
        step *= 2
    return e, ed


def combine(e, ed, x, xd, rate, length):
    rows = e.shape[0]
    incl, incld = scan(e, ed, rate, length)
    h, hd = lift(incl, 1), lift(incld, 1)
    back = ((rows - 1 - iota(x.shape, 0)) * length).astype(F32)
    fade = jnp.exp(-rate * back)
    x_all = jnp.sum(fade * x, axis=0, keepdims=True)
    xd_all = jnp.sum(fade * (xd + back * x), axis=0, keepdims=True)
    p = jnp.sum(x * h, axis=0, keepdims=True)
    pd = jnp.sum(xd * h + x * hd, axis=0, keepdims=True)
    return h, incl[0:1], incld[0:1], x_all, xd_all, p, pd


def pick(array, row):
    return jnp.sum(jnp.where(iota(array.shape, 0) == row, array, 0.0), axis=0, keepdims=True)


def tile(*rows):
    return jnp.concatenate(rows + (jnp.zeros((8 - len(rows), LANES), F32),), axis=0)


def kernel(
    ctx_n, chan_n,
    x_ref, g_ref, res_ref, rate_ref, y_ref, dres_ref, drate_ref,
    rows_x, rows_g, rows_y, corr_ref, par, mid, top,
    par_send, par_recv, mid_send, mid_recv, top_send, top_recv,
):
    ctx, chan = lax.axis_index("ctx"), lax.axis_index("chan")
    channels, span = x_ref.shape
    modes = res_ref.shape[1]
    chunks = span // LANES

    barrier = pltpu.get_barrier_semaphore()
    for r in range(1, chan_n):
        pl.semaphore_signal(
            barrier, inc=1, device_id={"chan": lax.rem(chan + r, chan_n)}, device_id_type=MESH
        )
    for r in range(1, ctx_n):
        pl.semaphore_signal(
            barrier, inc=1, device_id={"ctx": lax.rem(ctx + r, ctx_n)}, device_id_type=MESH
        )

    def exchange(buf, axis, me, n, send, recv):
        copies = []
        for r in range(1, n):
            copies.append(
                pltpu.make_async_remote_copy(
                    src_ref=buf.at[me],
                    dst_ref=buf.at[me],
                    send_sem=send.at[r],
                    recv_sem=recv.at[r],
                    device_id={axis: lax.rem(me + r, n)},
                    device_id_type=MESH,
                )
            )
        for copy in copies:
            copy.start()
        return copies

    repeats = LANES // modes
    par[chan] = tile(
        jnp.concatenate([res_ref[...]] * repeats, axis=1),
        jnp.concatenate([rate_ref[...]] * repeats, axis=1),
    )

    for n in range(chunks):
        rows_x[n * channels : (n + 1) * channels, :] = x_ref[:, n * LANES : (n + 1) * LANES].astype(F32)
        rows_g[n * channels : (n + 1) * channels, :] = g_ref[:, n * LANES : (n + 1) * LANES].astype(F32)
    xs = [rows_x[pl.ds(c, chunks, stride=channels), :].astype(BF16) for c in range(channels)]
    gs = [rows_g[pl.ds(c, chunks, stride=channels), :].astype(BF16) for c in range(channels)]
    down, across = iota((LANES, LANES), 0), iota((LANES, LANES), 1)
    lane8 = iota((8, LANES), 1)
    for c in range(channels):
        gram = lax.dot_general(xs[c], gs[c], (((0,), (0,)), ((), ())), preferred_element_type=F32)
        lags = gram[:8]
        for b in range(8, LANES, 8):
            moved = pltpu.roll(gram[b : b + 8], LANES - b, axis=1)
            lags += jnp.where(lane8 < LANES - b, moved, 0.0)
        corr_ref[c * 8 : (c + 1) * 8, :] = lags
    corr = corr_ref[pl.ds(0, channels, stride=8), :]
    for i in range(1, 8):
        moved = pltpu.roll(corr_ref[pl.ds(i, channels, stride=8), :], LANES - i, axis=1)
        corr += jnp.where(lane8 < LANES - i, moved, 0.0)

    pl.semaphore_wait(barrier, chan_n - 1 + ctx_n - 1)
    par_copies = exchange(par, "chan", chan, chan_n, par_send, par_recv)
    for copy in par_copies:
        copy.wait_recv()

    res8, rate8 = par[:, 0, :], par[:, 1, :]
    own = iota((chan_n, LANES), 1) // modes == iota((chan_n, LANES), 0)
    res = jnp.sum(jnp.where(own, res8, 0.0), axis=0, keepdims=True)
    rate = jnp.sum(jnp.where(own, rate8, 0.0), axis=0, keepdims=True)
    root = jnp.sqrt(rate)
    amp = res * root

    at = down.astype(F32)
    till = (LANES - down).astype(F32)
    decay_g, decay_x = jnp.exp(-rate * at), jnp.exp(-rate * till)

    def table(plain, weight):
        parts = split(plain), split(weight * plain)
        return jnp.concatenate(
            [jnp.concatenate([p[i] for p in parts], axis=1) for i in range(2)], axis=0
        )

    def twice(value):
        return jnp.concatenate([value, value], axis=1)

    corr_high, corr_low = split(corr)
    left_g = twice(jnp.concatenate(gs + [corr_high, corr_low], axis=0))
    left_x = twice(jnp.concatenate(xs, axis=0))
    raw_g = jnp.dot(left_g, table(decay_g, at), preferred_element_type=F32)
    raw_x = jnp.dot(left_x, table(decay_x, till), preferred_element_type=F32)
    lane_chan = iota((chunks, LANES), 1) // modes

    def by_channel(raw):
        plain = jnp.zeros((chunks, LANES), F32)
        weighted = plain
        for c in range(channels):
            part = raw[c * chunks : (c + 1) * chunks]
            plain = jnp.where(lane_chan == c, part[:, :LANES], plain)
            weighted = jnp.where(lane_chan == c, part[:, LANES:], weighted)
        return plain, weighted

    e, ed = by_channel(raw_g)
    x, xd = by_channel(raw_x)
    corr_rows = raw_g[channels * chunks :]
    corr_rows = corr_rows[:channels] + corr_rows[channels:]
    p_in = jnp.sum(jnp.where(own, corr_rows[:, :LANES], 0.0), axis=0, keepdims=True)
    pd_in = jnp.sum(jnp.where(own, corr_rows[:, LANES:], 0.0), axis=0, keepdims=True)

    h, e1, ed1, x1, xd1, p1, pd1 = combine(e, ed, x, xd, rate, LANES)
    mid[chan] = tile(e1, ed1, x1, xd1, p1 + p_in, pd1 + pd_in)
    mid_copies = exchange(mid, "chan", chan, chan_n, mid_send, mid_recv)

    lag = jnp.where(across[:channels] == 0, 0, LANES - across[:channels]).astype(F32)
    amp8 = res8 * jnp.sqrt(rate8)
    samples = jnp.zeros((channels, LANES), F32)
    for k in range(modes):
        samples += amp8[:, k : k + 1] * jnp.exp(-rate8[:, k : k + 1] * lag)
    for c in range(channels):
        spread = jnp.broadcast_to(samples[c : c + 1, :], (LANES, LANES))
        toeplitz = pltpu.roll(spread, 0, axis=1, stride=1, stride_axis=0)
        toeplitz = jnp.where(across <= down, toeplitz, 0.0)
        inner = jnp.dot(
            twice(gs[c]), jnp.concatenate(split(toeplitz), axis=0), preferred_element_type=F32
        )
        rows_y[c * chunks : (c + 1) * chunks, :] = inner

    for copy in mid_copies:
        copy.wait_recv()
    h2, e2, ed2, x2, xd2, p2, pd2 = combine(
        mid[:, 0, :], mid[:, 1, :], mid[:, 2, :], mid[:, 3, :], rate, span
    )
    p2 += jnp.sum(mid[:, 4, :], axis=0, keepdims=True)
    pd2 += jnp.sum(mid[:, 5, :], axis=0, keepdims=True)
    top[ctx] = tile(e2, ed2, x2, xd2, p2, pd2)
    top_copies = exchange(top, "ctx", ctx, ctx_n, top_send, top_recv)

    enter = pick(h2, chan)
    to_group_end = ((chan_n - 1 - chan) * span).astype(F32)
    group_fade = jnp.exp(-rate * to_group_end)
    to_end = ((chunks - 1 - iota((chunks, LANES), 0)) * LANES).astype(F32)
    chunk_fade = jnp.exp(-rate * to_end)
    out_high, out_low = split(amp * decay_x)
    out_table = jnp.concatenate(
        [twice(out_high), jnp.concatenate([out_low, jnp.zeros_like(out_low)], axis=1)], axis=0
    )

    for copy in top_copies:
        copy.wait_recv()
    h3, e3, ed3, x3, xd3, p3, pd3 = combine(
        top[:, 0, :], top[:, 1, :], top[:, 2, :], top[:, 3, :], rate, chan_n * span
    )
    enter = enter + group_fade * pick(h3, ctx)
    h = h + chunk_fade * enter
    lefts = []
    for c in range(channels):
        lefts.append(jnp.concatenate(split(jnp.where(lane_chan == c, h, 0.0)), axis=1))
    outer = lax.dot_general(
        jnp.concatenate(lefts, axis=0),
        out_table,
        (((1,), (1,)), ((), ())),
        preferred_element_type=F32,
    )
    total = rows_y[...] + outer[:, :LANES] + outer[:, LANES:]
    for c in range(channels):
        rows_g[pl.ds(c, chunks, stride=channels), :] = total[c * chunks : (c + 1) * chunks]
    for n in range(chunks):
        y_ref[:, n * LANES : (n + 1) * LANES] = rows_g[n * channels : (n + 1) * channels, :].astype(
            BF16
        )

    p3 += jnp.sum(top[:, 4, :], axis=0, keepdims=True)
    pd3 += jnp.sum(top[:, 5, :], axis=0, keepdims=True)
    final = tile(root * p3, amp * (0.5 * p3 - rate * pd3))
    final = pltpu.roll(final, lax.rem(LANES - modes * chan, LANES), axis=1)
    dres_ref[...] = final[0:1, :modes]
    drate_ref[...] = final[1:2, :modes]

    for copy in par_copies + mid_copies + top_copies:
        copy.wait_send()


def solution(mesh):
    ctx_n, chan_n = mesh.shape["ctx"], mesh.shape["chan"]

    def on_device(signal, grad_out, residue, decay_rate):
        channels, span = signal.shape
        modes = residue.shape[1]
        count = channels * span // LANES
        vmem = pl.BlockSpec(memory_space=pltpu.VMEM)
        small = jax.ShapeDtypeStruct((1, modes), F32)
        return pl.pallas_call(
            functools.partial(kernel, ctx_n, chan_n),
            out_shape=(jax.ShapeDtypeStruct((channels, span), BF16), small, small),
            in_specs=[vmem] * 4,
            out_specs=(vmem,) * 3,
            scratch_shapes=[
                pltpu.VMEM((count, LANES), F32),
                pltpu.VMEM((count, LANES), F32),
                pltpu.VMEM((count, LANES), F32),
                pltpu.VMEM((channels * 8, LANES), F32),
                pltpu.VMEM((chan_n, 8, LANES), F32),
                pltpu.VMEM((chan_n, 8, LANES), F32),
                pltpu.VMEM((ctx_n, 8, LANES), F32),
                pltpu.SemaphoreType.DMA((chan_n,)),
                pltpu.SemaphoreType.DMA((chan_n,)),
                pltpu.SemaphoreType.DMA((chan_n,)),
                pltpu.SemaphoreType.DMA((chan_n,)),
                pltpu.SemaphoreType.DMA((ctx_n,)),
                pltpu.SemaphoreType.DMA((ctx_n,)),
            ],
            compiler_params=pltpu.CompilerParams(
                collective_id=0, has_side_effects=True, vmem_limit_bytes=32 * 2**20
            ),
        )(signal, grad_out, residue, decay_rate)

    return jax.shard_map(
        on_device,
        mesh=mesh,
        in_specs=(
            P(None, ("ctx", "chan")),
            P(None, ("ctx", "chan")),
            P("chan", None),
            P("chan", None),
        ),
        out_specs=(P(None, ("ctx", "chan")), P("chan", None), P("chan", None)),
        check_vma=False,
    )
```

time: 1340 us -> 25.6 us (0.02)
  local copies, waits for them, and re-layouts: 743 us -> 4.63 us
  other arithmetic: 443 us -> 0 us
  blocking collectives: 53.2 us -> 0 us
  starting transfers between devices: 34.9 us -> 0 us
  matrix products: 29 us -> 0 us
  waiting for transfers between devices: 22.3 us -> 0 us
  Pallas kernels: 0 us -> 20.1 us
    unnamed x3 -> x0, other arithmetic: 426 us -> none
    all_to_all x4 -> x0, local copies, waits for them, and re-layouts: 355 us -> none  [the longest x1 245 us: on_device(): lax.all_to_all(filter_rows.reshape(chan_rows, 1, seq_block).astype(jnp.bf...]
    unnamed x22 -> x11, local copies, waits for them, and re-layouts: 301 us -> 4.63 us
    another operation x6 -> x0, local copies, waits for them, and re-layouts: 58.9 us -> none  [the longest x2 55.1 us: rotate(): return jnp.stack([real_part, imag_part])]
    all_to_all x5 -> x0, starting transfers between devices: 34.9 us -> none  [the longest x1 8.94 us: on_device(): lax.all_to_all(grad_rows, 'chan', split_axis=1, concat_axis=0, tiled=True)]
    psum x1 -> x0, blocking collectives: 30.1 us -> none  [on_device(): residue_grad, lograte_grad = lax.psum((residue_part, lograte_part), 'ctx')]
    dot_general x15 -> x0, matrix products: 29 us -> none  [the longest x4 8.86 us: dft_section(): with_sin = jnp.einsum(pattern, stacked, sines, precision=highest)]
    reshape x1 -> x0, local copies, waits for them, and re-layouts: 25.3 us -> none  [on_device(): laid_out.reshape(2, chan_rows, 1, seq_block)]
  transfers between devices with their start and end apart: 5 -> 0, of which waited for: 2 -> 0; matrix products, arithmetic and copies ran while one was open for 21% -> 0% of each run, Pallas kernels for 0% -> 0%
where the time goes in v1:
time: 25.6 us; the launch traced here: 25.4 us
  Pallas kernels  20.1 us (79%)
  local copies, waits for them, and re-layouts  4.63 us (18%)
  between operations  0.65 us (3%)
    pallas_call x1, Pallas kernels, on_device(): pl.pallas_call(functools.partial(kernel, ctx_n, chan_n), out_shape=(jax.S...  20.1 us
    unnamed x11, local copies, waits for them, and re-layouts  4.63 us

profile of v1, /device:TPU:1, one launch (start us, length us, event | category | flops | bytes accessed | tf_op | source)
XLA Modules:
  0.0 25.4 jit_solution(5865014097953184140)
XLA Ops:
  0.6 0.0 copy-start
  0.6 0.8 %copy-done = bf16[8,4096]{1,0:T(8,128)(2,1)S(1)} copy-done((bf16[8,4096]{1,0:T(8,128)(2,1)S(1)}, bf16[8,4096]{1,0:T(8,128)(2,1)}, u32[]{:S(2)}) %copy-start) | copy-done | bytes 65560
  1.5 0.0 copy-start.1
  1.5 0.8 %copy-done.1 = bf16[8,4096]{1,0:T(8,128)(2,1)S(1)} copy-done((bf16[8,4096]{1,0:T(8,128)(2,1)S(1)}, bf16[8,4096]{1,0:T(8,128)(2,1)}, u32[]{:S(2)}) %copy-start.1) | copy-done | bytes 65560
  2.3 0.0 copy-start.2
  2.3 0.7 %copy-done.2 = f32[1,16]{1,0:T(1,128)S(1)} copy-done((f32[1,16]{1,0:T(1,128)S(1)}, f32[1,16]{1,0:T(1,128)}, u32[]{:S(2)}) %copy-start.2) | copy-done | bytes 88
  3.0 0.0 copy-start.3
  3.0 0.7 %copy-done.3 = f32[1,16]{1,0:T(1,128)S(1)} copy-done((f32[1,16]{1,0:T(1,128)S(1)}, f32[1,16]{1,0:T(1,128)}, u32[]{:S(2)}) %copy-start.3) | copy-done | bytes 88
  3.6 20.1 %shard_map.67 = (bf16[8,4096]{1,0:T(8,128)(2,1)S(1)}, f32[1,16]{1,0:T(1,128)S(1)}, f32[1,16]{1,0:T(1,128)S(1)}) custom-call(bf16[8,4096]{1,0:T(8,128)(2,1)S(1)} %copy-done, bf16[8,4096]{1,0:T(8,128)(2,1)S(1)} %copy-done.1, f32[1,16]{1,0:T(1,128)S(1)} %copy-done.2, f32[1,16]{1,0:T(1,128)S(1)} %copy-done.3), custom_call_target="tpu_custom_call" | custom-call | tf_op jit(solution)/shard_map/pallas_call | solution.py:256
  23.7 0.6 %copy.10 = bf16[8,4096]{1,0:T(8,128)(2,1)} copy(bf16[8,4096]{1,0:T(8,128)(2,1)S(1)} %get-tuple-element.6) | data formatting | bytes 131072
  24.3 0.5 %copy.11 = f32[1,16]{1,0:T(1,128)} copy(f32[1,16]{1,0:T(1,128)S(1)} %get-tuple-element.7) | data formatting | bytes 128
  24.9 0.5 %copy.12 = f32[1,16]{1,0:T(1,128)} copy(f32[1,16]{1,0:T(1,128)S(1)} %get-tuple-element.8) | data formatting | bytes 128
Async XLA Ops:
  0.6 0.8 %copy-start = (bf16[8,4096]{1,0:T(8,128)(2,1)S(1)}, bf16[8,4096]{1,0:T(8,128)(2,1)}, u32[]{:S(2)}) copy-start(bf16[8,4096]{1,0:T(8,128)(2,1)} %x_ref.1) | copy-start | bytes 196612
  1.5 0.8 %copy-start.1 = (bf16[8,4096]{1,0:T(8,128)(2,1)S(1)}, bf16[8,4096]{1,0:T(8,128)(2,1)}, u32[]{:S(2)}) copy-start(bf16[8,4096]{1,0:T(8,128)(2,1)} %g_ref.1) | copy-start | bytes 196612
  2.3 0.7 %copy-start.2 = (f32[1,16]{1,0:T(1,128)S(1)}, f32[1,16]{1,0:T(1,128)}, u32[]{:S(2)}) copy-start(f32[1,16]{1,0:T(1,128)} %res_ref.1) | copy-start | bytes 196
  3.0 0.7 %copy-start.3 = (f32[1,16]{1,0:T(1,128)S(1)}, f32[1,16]{1,0:T(1,128)}, u32[]{:S(2)}) copy-start(f32[1,16]{1,0:T(1,128)} %rate_ref.1) | copy-start | bytes 196

commit v2 on v1

--- a/solution.py
+++ b/solution.py
@@ -52,25 +52,26 @@
     return h, incl[0:1], incld[0:1], x_all, xd_all, p, pd
 
 
-def pick(array, row):
-    return jnp.sum(jnp.where(iota(array.shape, 0) == row, array, 0.0), axis=0, keepdims=True)
-
-
-def tile(*rows):
-    return jnp.concatenate(rows + (jnp.zeros((8 - len(rows), LANES), F32),), axis=0)
-
-
 def kernel(
     ctx_n, chan_n,
-    x_ref, g_ref, res_ref, rate_ref, y_ref, dres_ref, drate_ref,
-    rows_x, rows_g, rows_y, corr_ref, par, mid, top,
-    par_send, par_recv, mid_send, mid_recv, top_send, top_recv,
+    x_hbm, g_hbm, res_hbm, rate_hbm, y_ref, dres_ref, drate_ref,
+    rows_x, rows_g, rows_y, corr_ref, par, out_stats, stats,
+    x_ref, g_ref, res_ref, rate_ref, load_sem,
+    par_send, par_recv, stats_send, stats_recv,
 ):
     ctx, chan = lax.axis_index("ctx"), lax.axis_index("chan")
     channels, span = x_ref.shape
     modes = res_ref.shape[1]
     chunks = span // LANES
 
+    loads = [
+        pltpu.make_async_copy(source, target, load_sem.at[i])
+        for i, (source, target) in enumerate(
+            [(res_hbm, res_ref), (rate_hbm, rate_ref), (x_hbm, x_ref), (g_hbm, g_ref)]
+        )
+    ]
+    for load in loads:
+        load.start()
     barrier = pltpu.get_barrier_semaphore()
     for r in range(1, chan_n):
         pl.semaphore_signal(
@@ -98,12 +99,14 @@
             copy.start()
         return copies
 
+    loads[0].wait()
+    loads[1].wait()
     repeats = LANES // modes
-    par[chan] = tile(
-        jnp.concatenate([res_ref[...]] * repeats, axis=1),
-        jnp.concatenate([rate_ref[...]] * repeats, axis=1),
-    )
-
+    par[chan, 0:1, :] = jnp.concatenate([res_ref[...]] * repeats, axis=1)
+    par[chan, 1:2, :] = jnp.concatenate([rate_ref[...]] * repeats, axis=1)
+
+    loads[2].wait()
+    loads[3].wait()
     for n in range(chunks):
         rows_x[n * channels : (n + 1) * channels, :] = x_ref[:, n * LANES : (n + 1) * LANES].astype(F32)
         rows_g[n * channels : (n + 1) * channels, :] = g_ref[:, n * LANES : (n + 1) * LANES].astype(F32)
@@ -172,8 +175,32 @@
     pd_in = jnp.sum(jnp.where(own, corr_rows[:, LANES:], 0.0), axis=0, keepdims=True)
 
     h, e1, ed1, x1, xd1, p1, pd1 = combine(e, ed, x, xd, rate, LANES)
-    mid[chan] = tile(e1, ed1, x1, xd1, p1 + p_in, pd1 + pd_in)
-    mid_copies = exchange(mid, "chan", chan, chan_n, mid_send, mid_recv)
+    sums = [e1, ed1, x1, xd1, p1 + p_in, pd1 + pd_in]
+    owner_row = iota((chan_n, LANES), 0)
+    lane_group = iota((chan_n, LANES), 1) // modes
+    for_owner = jnp.zeros((chan_n, LANES), F32)
+    for q, value in enumerate(sums):
+        moved = pltpu.roll(value, modes * q, axis=1) if q else value
+        for_owner = jnp.where(lane_group == (owner_row + q) % chan_n, moved, for_owner)
+    out_stats[:, 0, :] = jnp.broadcast_to(e1, (chan_n, LANES))
+    out_stats[:, 1, :] = for_owner
+    count = ctx_n * chan_n
+    me = ctx * chan_n + chan
+
+    @pl.loop(0, count - 1)
+    def _(i):
+        to = i + jnp.where(i >= me, 1, 0)
+        to_chan = lax.rem(to, chan_n)
+        pltpu.make_async_remote_copy(
+            src_ref=out_stats.at[to_chan],
+            dst_ref=stats.at[me],
+            send_sem=stats_send,
+            recv_sem=stats_recv,
+            device_id={"ctx": lax.div(to, chan_n), "chan": to_chan},
+            device_id_type=MESH,
+        ).start()
+
+    stats[me] = out_stats[chan]
 
     lag = jnp.where(across[:channels] == 0, 0, LANES - across[:channels]).astype(F32)
     amp8 = res8 * jnp.sqrt(rate8)
@@ -189,32 +216,19 @@
         )
         rows_y[c * chunks : (c + 1) * chunks, :] = inner
 
-    for copy in mid_copies:
-        copy.wait_recv()
-    h2, e2, ed2, x2, xd2, p2, pd2 = combine(
-        mid[:, 0, :], mid[:, 1, :], mid[:, 2, :], mid[:, 3, :], rate, span
-    )
-    p2 += jnp.sum(mid[:, 4, :], axis=0, keepdims=True)
-    pd2 += jnp.sum(mid[:, 5, :], axis=0, keepdims=True)
-    top[ctx] = tile(e2, ed2, x2, xd2, p2, pd2)
-    top_copies = exchange(top, "ctx", ctx, ctx_n, top_send, top_recv)
-
-    enter = pick(h2, chan)
-    to_group_end = ((chan_n - 1 - chan) * span).astype(F32)
-    group_fade = jnp.exp(-rate * to_group_end)
     to_end = ((chunks - 1 - iota((chunks, LANES), 0)) * LANES).astype(F32)
     chunk_fade = jnp.exp(-rate * to_end)
     out_high, out_low = split(amp * decay_x)
     out_table = jnp.concatenate(
         [twice(out_high), jnp.concatenate([out_low, jnp.zeros_like(out_low)], axis=1)], axis=0
     )
-
-    for copy in top_copies:
-        copy.wait_recv()
-    h3, e3, ed3, x3, xd3, p3, pd3 = combine(
-        top[:, 0, :], top[:, 1, :], top[:, 2, :], top[:, 3, :], rate, chan_n * span
-    )
-    enter = enter + group_fade * pick(h3, ctx)
+    ahead = iota((count, LANES), 0) - (me + 1)
+    fade_in = jnp.exp(-rate * (jnp.maximum(ahead, 0) * span).astype(F32))
+    fade_in = jnp.where(ahead >= 0, fade_in, 0.0)
+
+    everyone = stats.at[pl.ds(0, count - 1)]
+    pltpu.make_async_copy(everyone, everyone, stats_recv).wait()
+    enter = jnp.sum(fade_in * stats[:, 0, :], axis=0, keepdims=True)
     h = h + chunk_fade * enter
     lefts = []
     for c in range(channels):
@@ -233,14 +247,20 @@
             BF16
         )
 
-    p3 += jnp.sum(top[:, 4, :], axis=0, keepdims=True)
-    pd3 += jnp.sum(top[:, 5, :], axis=0, keepdims=True)
-    final = tile(root * p3, amp * (0.5 * p3 - rate * pd3))
-    final = pltpu.roll(final, lax.rem(LANES - modes * chan, LANES), axis=1)
-    dres_ref[...] = final[0:1, :modes]
-    drate_ref[...] = final[1:2, :modes]
-
-    for copy in par_copies + mid_copies + top_copies:
+    mine = stats[:, 1, :]
+    groups = [
+        pltpu.roll(mine, lax.rem(2 * LANES - modes * (chan + q), LANES), axis=1) for q in range(6)
+    ]
+    own_res, own_rate = par[chan, 0:1, :], par[chan, 1:2, :]
+    *_, plain, tilted = combine(*groups[:4], own_rate, span)
+    plain += jnp.sum(groups[4], axis=0, keepdims=True)
+    tilted += jnp.sum(groups[5], axis=0, keepdims=True)
+    own_root = jnp.sqrt(own_rate)
+    dres_ref[...] = (own_root * plain)[:, :modes]
+    drate_ref[...] = (own_res * own_root * (0.5 * plain - own_rate * tilted))[:, :modes]
+
+    pltpu.make_async_copy(everyone, everyone, stats_send).wait()
+    for copy in par_copies:
         copy.wait_send()
 
 
@@ -256,25 +276,28 @@
         return pl.pallas_call(
             functools.partial(kernel, ctx_n, chan_n),
             out_shape=(jax.ShapeDtypeStruct((channels, span), BF16), small, small),
-            in_specs=[vmem] * 4,
+            in_specs=[pl.BlockSpec(memory_space=pl.ANY)] * 4,
             out_specs=(vmem,) * 3,
             scratch_shapes=[
                 pltpu.VMEM((count, LANES), F32),
                 pltpu.VMEM((count, LANES), F32),
                 pltpu.VMEM((count, LANES), F32),
                 pltpu.VMEM((channels * 8, LANES), F32),
-                pltpu.VMEM((chan_n, 8, LANES), F32),
-                pltpu.VMEM((chan_n, 8, LANES), F32),
-                pltpu.VMEM((ctx_n, 8, LANES), F32),
+                pltpu.VMEM((chan_n, 2, LANES), F32),
+                pltpu.VMEM((chan_n, 2, LANES), F32),
+                pltpu.VMEM((ctx_n * chan_n, 2, LANES), F32),
+                pltpu.VMEM((channels, span), BF16),
+                pltpu.VMEM((channels, span), BF16),
+                pltpu.VMEM((1, modes), F32),
+                pltpu.VMEM((1, modes), F32),
+                pltpu.SemaphoreType.DMA((4,)),
                 pltpu.SemaphoreType.DMA((chan_n,)),
                 pltpu.SemaphoreType.DMA((chan_n,)),
-                pltpu.SemaphoreType.DMA((chan_n,)),
-                pltpu.SemaphoreType.DMA((chan_n,)),
-                pltpu.SemaphoreType.DMA((ctx_n,)),
-                pltpu.SemaphoreType.DMA((ctx_n,)),
+                pltpu.SemaphoreType.DMA,
+                pltpu.SemaphoreType.DMA,
             ],
             compiler_params=pltpu.CompilerParams(
-                collective_id=0, has_side_effects=True, vmem_limit_bytes=32 * 2**20
+                collective_id=0, has_side_effects=True, vmem_limit_bytes=60 * 2**20
             ),
         )(signal, grad_out, residue, decay_rate)
 

time: 25.6 us -> 22.1 us (0.86)
  local copies, waits for them, and re-layouts: 4.63 us -> 2.58 us
  Pallas kernels: 20.1 us -> 18.6 us
    unnamed x11 -> x7, local copies, waits for them, and re-layouts: 4.63 us -> 2.58 us
    pallas_call x1, Pallas kernels: 20.1 us -> 18.6 us  [on_device(): pl.pallas_call(functools.partial(kernel, ctx_n, chan_n), out_shape=(jax.S...]
where the time goes in v2:
time: 22.1 us; the launch traced here: 21.9 us
  Pallas kernels  18.6 us (84%)
  local copies, waits for them, and re-layouts  2.58 us (12%)
  between operations  0.65 us (3%)
    pallas_call x1, Pallas kernels, on_device(): pl.pallas_call(functools.partial(kernel, ctx_n, chan_n), out_shape=(jax.S...  18.6 us
    unnamed x7, local copies, waits for them, and re-layouts  2.58 us

profile of v2, /device:TPU:1, one launch (start us, length us, event | category | flops | bytes accessed | tf_op | source)
XLA Modules:
  0.0 21.9 jit_solution(6278560093935480695)
XLA Ops:
  0.6 18.6 %shard_map.67 = (bf16[8,4096]{1,0:T(8,128)(2,1)}, f32[1,16]{1,0:T(1,128)}, f32[1,16]{1,0:T(1,128)}) custom-call(bf16[8,4096]{1,0:T(8,128)(2,1)} %x_hbm.1, bf16[8,4096]{1,0:T(8,128)(2,1)} %g_hbm.1, f32[1,16]{1,0:T(1,128)} %res_hbm.1, f32[1,16]{1,0:T(1,128)} %rate_hbm.1), custom_call_target="tpu_custom_call" | custom-call | tf_op jit(solution)/shard_map/pallas_call | solution.py:276
  19.3 0.0 copy-start.1
  19.3 1.5 %copy.10 = bf16[8,4096]{1,0:T(8,128)(2,1)} copy(bf16[8,4096]{1,0:T(8,128)(2,1)} %get-tuple-element.6) | data formatting | bytes 131072
  20.8 0.0 copy-done.1
  20.8 0.0 copy-start
  20.8 0.5 %copy.11 = f32[1,16]{1,0:T(1,128)} copy(f32[1,16]{1,0:T(1,128)S(1)} %copy-done.1) | data formatting | bytes 128
  21.3 0.1 copy-done
  21.4 0.5 %copy.12 = f32[1,16]{1,0:T(1,128)} copy(f32[1,16]{1,0:T(1,128)S(1)} %copy-done) | data formatting | bytes 128
Async XLA Ops:
  19.3 1.5 %copy-start.1 = (f32[1,16]{1,0:T(1,128)S(1)}, f32[1,16]{1,0:T(1,128)}, u32[]{:S(2)}) copy-start(f32[1,16]{1,0:T(1,128)} %get-tuple-element.7) | copy-start | bytes 196
  20.8 0.6 %copy-start = (f32[1,16]{1,0:T(1,128)S(1)}, f32[1,16]{1,0:T(1,128)}, u32[]{:S(2)}) copy-start(f32[1,16]{1,0:T(1,128)} %get-tuple-element.8) | copy-start | bytes 196

commit v3 on v2

--- a/solution.py
+++ b/solution.py
@@ -54,7 +54,7 @@
 
 def kernel(
     ctx_n, chan_n,
-    x_hbm, g_hbm, res_hbm, rate_hbm, y_ref, dres_ref, drate_ref,
+    x_hbm, g_hbm, res_hbm, rate_hbm, y_ref, small_ref,
     rows_x, rows_g, rows_y, corr_ref, par, out_stats, stats,
     x_ref, g_ref, res_ref, rate_ref, load_sem,
     par_send, par_recv, stats_send, stats_recv,
@@ -256,8 +256,8 @@
     plain += jnp.sum(groups[4], axis=0, keepdims=True)
     tilted += jnp.sum(groups[5], axis=0, keepdims=True)
     own_root = jnp.sqrt(own_rate)
-    dres_ref[...] = (own_root * plain)[:, :modes]
-    drate_ref[...] = (own_res * own_root * (0.5 * plain - own_rate * tilted))[:, :modes]
+    small_ref[0:1, :] = own_root * plain
+    small_ref[1:2, :] = own_res * own_root * (0.5 * plain - own_rate * tilted)
 
     pltpu.make_async_copy(everyone, everyone, stats_send).wait()
     for copy in par_copies:
@@ -271,13 +271,14 @@
         channels, span = signal.shape
         modes = residue.shape[1]
         count = channels * span // LANES
+        pinned = [pltpu.with_memory_space_constraint(v, pltpu.HBM) for v in (signal, grad_out, residue, decay_rate)]
         vmem = pl.BlockSpec(memory_space=pltpu.VMEM)
-        small = jax.ShapeDtypeStruct((1, modes), F32)
-        return pl.pallas_call(
+        small = jax.ShapeDtypeStruct((2, LANES), F32)
+        y, small = pl.pallas_call(
             functools.partial(kernel, ctx_n, chan_n),
-            out_shape=(jax.ShapeDtypeStruct((channels, span), BF16), small, small),
+            out_shape=(jax.ShapeDtypeStruct((channels, span), BF16), small),
             in_specs=[pl.BlockSpec(memory_space=pl.ANY)] * 4,
-            out_specs=(vmem,) * 3,
+            out_specs=(vmem,) * 2,
             scratch_shapes=[
                 pltpu.VMEM((count, LANES), F32),
                 pltpu.VMEM((count, LANES), F32),
@@ -297,9 +298,10 @@
                 pltpu.SemaphoreType.DMA,
             ],
             compiler_params=pltpu.CompilerParams(
-                collective_id=0, has_side_effects=True, vmem_limit_bytes=60 * 2**20
+                collective_id=0, has_side_effects=True, vmem_limit_bytes=32 * 2**20
             ),
-        )(signal, grad_out, residue, decay_rate)
+        )(*pinned)
+        return y, small[0:1, :modes], small[1:2, :modes]
 
     return jax.shard_map(
         on_device,

time: 22.1 us -> 20 us (0.905)
  local copies, waits for them, and re-layouts: 2.58 us -> 1.15 us
  Pallas kernels: 18.6 us -> 18 us
    unnamed x7 -> x1, local copies, waits for them, and re-layouts: 2.58 us -> 0.63 us
    pallas_call x1, Pallas kernels: 18.6 us -> 18 us  [on_device(): pl.pallas_call(functools.partial(kernel, ctx_n, chan_n), out_shape=(jax.S...]
    slice x0 -> x1, local copies, waits for them, and re-layouts: none -> 0.52 us  [on_device(): return (y, small[0:1, :modes], small[1:2, :modes])]
where the time goes in v3:
time: 20 us; the launch traced here: 19.8 us
  Pallas kernels  18 us (90%)
  local copies, waits for them, and re-layouts  1.15 us (6%)
  between operations  0.64 us (3%)
    pallas_call x1, Pallas kernels, on_device(): pl.pallas_call(functools.partial(kernel, ctx_n, chan_n), out_shape=(jax.S...  18 us
    unnamed x1, local copies, waits for them, and re-layouts  0.63 us
    slice x1, local copies, waits for them, and re-layouts, on_device(): return (y, small[0:1, :modes], small[1:2, :modes])  0.52 us

profile of v3, /device:TPU:1, one launch (start us, length us, event | category | flops | bytes accessed | tf_op | source)
XLA Modules:
  0.0 19.8 jit_solution(16888942031702539825)
XLA Ops:
  0.6 18.0 %shard_map.67 = (bf16[8,4096]{1,0:T(8,128)(2,1)S(1)}, f32[2,128]{1,0:T(2,128)S(1)}) custom-call(bf16[8,4096]{1,0:T(8,128)(2,1)} %x_hbm.1, bf16[8,4096]{1,0:T(8,128)(2,1)} %g_hbm.1, f32[1,16]{1,0:T(1,128)} %res_hbm.1, f32[1,16]{1,0:T(1,128)} %rate_hbm.1), custom_call_target="tpu_custom_call" | custom-call | tf_op jit(solution)/shard_map/pallas_call | solution.py:277
  18.7 0.5 %fusion = (f32[1,16]{1,0:T(1,128)}, f32[1,16]{1,0:T(1,128)}) fusion(f32[2,128]{1,0:T(2,128)S(1)} %get-tuple-element.6), kind=kLoop, calls=%fused_computation | loop fusion | bytes 256 | tf_op jit(solution)/shard_map/slice | solution.py:304
  19.2 0.6 %copy.8 = bf16[8,4096]{1,0:T(8,128)(2,1)} copy(bf16[8,4096]{1,0:T(8,128)(2,1)S(1)} %get-tuple-element.12) | data formatting | bytes 131072

commit v4 on v3

--- a/solution.py
+++ b/solution.py
@@ -28,34 +28,26 @@
     return jnp.where(iota(array.shape, 0) < rows - step, moved, 0.0)
 
 
-def scan(e, ed, rate, length):
-    rows = e.shape[0]
-    step = 1
-    while step < rows:
-        fade = jnp.exp(-rate * float(step * length))
+def scan_fades(rate, rows, length):
+    return [jnp.exp(-rate * float(length << i)) for i in range((rows - 1).bit_length())]
+
+
+def entering(e, ed, fades, length):
+    for i, fade in enumerate(fades):
+        step = 1 << i
         up, upd = lift(e, step), lift(ed, step)
         e, ed = e + fade * up, ed + fade * (upd + float(step * length) * up)
-        step *= 2
-    return e, ed
-
-
-def combine(e, ed, x, xd, rate, length):
-    rows = e.shape[0]
-    incl, incld = scan(e, ed, rate, length)
-    h, hd = lift(incl, 1), lift(incld, 1)
-    back = ((rows - 1 - iota(x.shape, 0)) * length).astype(F32)
-    fade = jnp.exp(-rate * back)
-    x_all = jnp.sum(fade * x, axis=0, keepdims=True)
-    xd_all = jnp.sum(fade * (xd + back * x), axis=0, keepdims=True)
-    p = jnp.sum(x * h, axis=0, keepdims=True)
-    pd = jnp.sum(xd * h + x * hd, axis=0, keepdims=True)
-    return h, incl[0:1], incld[0:1], x_all, xd_all, p, pd
+    return lift(e, 1), lift(ed, 1), e[0:1], ed[0:1]
+
+
+def total_over(rows):
+    return jnp.sum(rows, axis=0, keepdims=True)
 
 
 def kernel(
     ctx_n, chan_n,
     x_hbm, g_hbm, res_hbm, rate_hbm, y_ref, small_ref,
-    rows_x, rows_g, rows_y, corr_ref, par, out_stats, stats,
+    rows_x, rows_g, rows_y, rows_f, corr_ref, par, out_stats, stats,
     x_ref, g_ref, res_ref, rate_ref, load_sem,
     par_send, par_recv, stats_send, stats_recv,
 ):
@@ -104,6 +96,9 @@
     repeats = LANES // modes
     par[chan, 0:1, :] = jnp.concatenate([res_ref[...]] * repeats, axis=1)
     par[chan, 1:2, :] = jnp.concatenate([rate_ref[...]] * repeats, axis=1)
+
+    pl.semaphore_wait(barrier, chan_n - 1 + ctx_n - 1)
+    par_copies = exchange(par, "chan", chan, chan_n, par_send, par_recv)
 
     loads[2].wait()
     loads[3].wait()
@@ -126,8 +121,6 @@
         moved = pltpu.roll(corr_ref[pl.ds(i, channels, stride=8), :], LANES - i, axis=1)
         corr += jnp.where(lane8 < LANES - i, moved, 0.0)
 
-    pl.semaphore_wait(barrier, chan_n - 1 + ctx_n - 1)
-    par_copies = exchange(par, "chan", chan, chan_n, par_send, par_recv)
     for copy in par_copies:
         copy.wait_recv()
 
@@ -138,6 +131,9 @@
     root = jnp.sqrt(rate)
     amp = res * root
 
+    chunk_fades = scan_fades(rate, chunks, LANES)
+    to_end = ((chunks - 1 - iota((chunks, LANES), 0)) * LANES).astype(F32)
+    chunk_fade = jnp.exp(-rate * to_end)
     at = down.astype(F32)
     till = (LANES - down).astype(F32)
     decay_g, decay_x = jnp.exp(-rate * at), jnp.exp(-rate * till)
@@ -174,8 +170,12 @@
     p_in = jnp.sum(jnp.where(own, corr_rows[:, :LANES], 0.0), axis=0, keepdims=True)
     pd_in = jnp.sum(jnp.where(own, corr_rows[:, LANES:], 0.0), axis=0, keepdims=True)
 
-    h, e1, ed1, x1, xd1, p1, pd1 = combine(e, ed, x, xd, rate, LANES)
-    sums = [e1, ed1, x1, xd1, p1 + p_in, pd1 + pd_in]
+    h, hd, e1, ed1 = entering(e, ed, chunk_fades, LANES)
+    x1 = total_over(chunk_fade * x)
+    xd1 = total_over(chunk_fade * (xd + to_end * x))
+    p1 = p_in + total_over(x * h)
+    pd1 = pd_in + total_over(xd * h + x * hd)
+    sums = [ed1, x1, xd1, p1, pd1]
     owner_row = iota((chan_n, LANES), 0)
     lane_group = iota((chan_n, LANES), 1) // modes
     for_owner = jnp.zeros((chan_n, LANES), F32)
@@ -207,6 +207,23 @@
     samples = jnp.zeros((channels, LANES), F32)
     for k in range(modes):
         samples += amp8[:, k : k + 1] * jnp.exp(-rate8[:, k : k + 1] * lag)
+    out_high, out_low = split(amp * decay_x)
+    out_table = jnp.concatenate(
+        [twice(out_high), jnp.concatenate([out_low, jnp.zeros_like(out_low)], axis=1)], axis=0
+    )
+
+    def expand(states):
+        outer = lax.dot_general(
+            jnp.concatenate(split(states), axis=1),
+            out_table,
+            (((1,), (1,)), ((), ())),
+            preferred_element_type=F32,
+        )
+        return outer[:, :LANES] + outer[:, LANES:]
+
+    local = expand(
+        jnp.concatenate([jnp.where(lane_chan == c, h, 0.0) for c in range(channels)], axis=0)
+    )
     for c in range(channels):
         spread = jnp.broadcast_to(samples[c : c + 1, :], (LANES, LANES))
         toeplitz = pltpu.roll(spread, 0, axis=1, stride=1, stride_axis=0)
@@ -214,50 +231,33 @@
         inner = jnp.dot(
             twice(gs[c]), jnp.concatenate(split(toeplitz), axis=0), preferred_element_type=F32
         )
-        rows_y[c * chunks : (c + 1) * chunks, :] = inner
-
-    to_end = ((chunks - 1 - iota((chunks, LANES), 0)) * LANES).astype(F32)
-    chunk_fade = jnp.exp(-rate * to_end)
-    out_high, out_low = split(amp * decay_x)
-    out_table = jnp.concatenate(
-        [twice(out_high), jnp.concatenate([out_low, jnp.zeros_like(out_low)], axis=1)], axis=0
-    )
+        rows_y[pl.ds(c, chunks, stride=channels), :] = inner + local[c * chunks : (c + 1) * chunks]
+
+    for n in range(chunks):
+        rows_x[n * channels : (n + 1) * channels, :] = jnp.where(own, chunk_fade[n : n + 1], 0.0)
     ahead = iota((count, LANES), 0) - (me + 1)
     fade_in = jnp.exp(-rate * (jnp.maximum(ahead, 0) * span).astype(F32))
-    fade_in = jnp.where(ahead >= 0, fade_in, 0.0)
+    rows_f[...] = jnp.where(ahead >= 0, fade_in, 0.0)
+    span_fades = scan_fades(rate, count, span)
 
     everyone = stats.at[pl.ds(0, count - 1)]
     pltpu.make_async_copy(everyone, everyone, stats_recv).wait()
-    enter = jnp.sum(fade_in * stats[:, 0, :], axis=0, keepdims=True)
-    h = h + chunk_fade * enter
-    lefts = []
-    for c in range(channels):
-        lefts.append(jnp.concatenate(split(jnp.where(lane_chan == c, h, 0.0)), axis=1))
-    outer = lax.dot_general(
-        jnp.concatenate(lefts, axis=0),
-        out_table,
-        (((1,), (1,)), ((), ())),
-        preferred_element_type=F32,
-    )
-    total = rows_y[...] + outer[:, :LANES] + outer[:, LANES:]
-    for c in range(channels):
-        rows_g[pl.ds(c, chunks, stride=channels), :] = total[c * chunks : (c + 1) * chunks]
+    states, mine = stats[:, 0, :], stats[:, 1, :]
+    enter = total_over(rows_f[...] * states)
+    y = rows_y[...] + expand(rows_x[...] * enter)
     for n in range(chunks):
-        y_ref[:, n * LANES : (n + 1) * LANES] = rows_g[n * channels : (n + 1) * channels, :].astype(
-            BF16
-        )
-
-    mine = stats[:, 1, :]
-    groups = [
-        pltpu.roll(mine, lax.rem(2 * LANES - modes * (chan + q), LANES), axis=1) for q in range(6)
-    ]
-    own_res, own_rate = par[chan, 0:1, :], par[chan, 1:2, :]
-    *_, plain, tilted = combine(*groups[:4], own_rate, span)
-    plain += jnp.sum(groups[4], axis=0, keepdims=True)
-    tilted += jnp.sum(groups[5], axis=0, keepdims=True)
-    own_root = jnp.sqrt(own_rate)
-    small_ref[0:1, :] = own_root * plain
-    small_ref[1:2, :] = own_res * own_root * (0.5 * plain - own_rate * tilted)
+        y_ref[:, n * LANES : (n + 1) * LANES] = y[n * channels : (n + 1) * channels].astype(BF16)
+
+    def shifted(value, q):
+        return pltpu.roll(value, LANES - modes * q, axis=1)
+
+    h, hd, _, _ = entering(states, mine, span_fades, span)
+    x, xd = shifted(mine, 1), shifted(mine, 2)
+    sums = total_over(mine)
+    plain = shifted(sums, 3) + total_over(x * h)
+    tilted = shifted(sums, 4) + total_over(xd * h + x * hd)
+    final = jnp.concatenate([root * plain, amp * (0.5 * plain - rate * tilted)], axis=0)
+    small_ref[...] = pltpu.roll(final, lax.rem(LANES - modes * chan, LANES), axis=1)
 
     pltpu.make_async_copy(everyone, everyone, stats_send).wait()
     for copy in par_copies:
@@ -283,6 +283,7 @@
                 pltpu.VMEM((count, LANES), F32),
                 pltpu.VMEM((count, LANES), F32),
                 pltpu.VMEM((count, LANES), F32),
+                pltpu.VMEM((ctx_n * chan_n, LANES), F32),
                 pltpu.VMEM((channels * 8, LANES), F32),
                 pltpu.VMEM((chan_n, 2, LANES), F32),
                 pltpu.VMEM((chan_n, 2, LANES), F32),

time: 20 us -> 19.9 us (level)
  no operation moved by 1% of the time
where the time goes in v4:
time: 19.9 us; the launch traced here: 19.7 us
  Pallas kernels  18 us (90%)
  local copies, waits for them, and re-layouts  1.15 us (6%)
  between operations  0.64 us (3%)
    pallas_call x1, Pallas kernels, on_device(): pl.pallas_call(functools.partial(kernel, ctx_n, chan_n), out_shape=(jax.S...  18 us
    unnamed x1, local copies, waits for them, and re-layouts  0.63 us
    slice x1, local copies, waits for them, and re-layouts, on_device(): return (y, small[0:1, :modes], small[1:2, :modes])  0.52 us

profile of v4, /device:TPU:1, one launch (start us, length us, event | category | flops | bytes accessed | tf_op | source)
XLA Modules:
  0.0 19.7 jit_solution(15351672774199309433)
XLA Ops:
  0.6 18.0 %shard_map.67 = (bf16[8,4096]{1,0:T(8,128)(2,1)S(1)}, f32[2,128]{1,0:T(2,128)S(1)}) custom-call(bf16[8,4096]{1,0:T(8,128)(2,1)} %x_hbm.1, bf16[8,4096]{1,0:T(8,128)(2,1)} %g_hbm.1, f32[1,16]{1,0:T(1,128)} %res_hbm.1, f32[1,16]{1,0:T(1,128)} %rate_hbm.1), custom_call_target="tpu_custom_call" | custom-call | tf_op jit(solution)/shard_map/pallas_call | solution.py:277
  18.6 0.5 %fusion = (f32[1,16]{1,0:T(1,128)}, f32[1,16]{1,0:T(1,128)}) fusion(f32[2,128]{1,0:T(2,128)S(1)} %get-tuple-element.6), kind=kLoop, calls=%fused_computation | loop fusion | bytes 256 | tf_op jit(solution)/shard_map/slice | solution.py:305
  19.1 0.6 %copy.8 = bf16[8,4096]{1,0:T(8,128)(2,1)} copy(bf16[8,4096]{1,0:T(8,128)(2,1)S(1)} %get-tuple-element.12) | data formatting | bytes 131072

commit v5 on v4

--- a/solution.py
+++ b/solution.py
@@ -38,6 +38,10 @@
         up, upd = lift(e, step), lift(ed, step)
         e, ed = e + fade * up, ed + fade * (upd + float(step * length) * up)
     return lift(e, 1), lift(ed, 1), e[0:1], ed[0:1]
+
+
+def farthest_first(n):
+    return sorted(range(1, n), key=lambda r: -min(r, n - r))
 
 
 def total_over(rows):
@@ -62,10 +66,10 @@
             [(res_hbm, res_ref), (rate_hbm, rate_ref), (x_hbm, x_ref), (g_hbm, g_ref)]
         )
     ]
-    for load in loads:
-        load.start()
+    loads[0].start()
+    loads[1].start()
     barrier = pltpu.get_barrier_semaphore()
-    for r in range(1, chan_n):
+    for r in farthest_first(chan_n):
         pl.semaphore_signal(
             barrier, inc=1, device_id={"chan": lax.rem(chan + r, chan_n)}, device_id_type=MESH
         )
@@ -73,23 +77,24 @@
         pl.semaphore_signal(
             barrier, inc=1, device_id={"ctx": lax.rem(ctx + r, ctx_n)}, device_id_type=MESH
         )
+    loads[2].start()
+    loads[3].start()
 
     def exchange(buf, axis, me, n, send, recv):
         copies = []
-        for r in range(1, n):
+        for r in farthest_first(n):
             copies.append(
                 pltpu.make_async_remote_copy(
                     src_ref=buf.at[me],
                     dst_ref=buf.at[me],
-                    send_sem=send.at[r],
-                    recv_sem=recv.at[r],
+                    send_sem=send,
+                    recv_sem=recv,
                     device_id={axis: lax.rem(me + r, n)},
                     device_id_type=MESH,
                 )
             )
         for copy in copies:
             copy.start()
-        return copies
 
     loads[0].wait()
     loads[1].wait()
@@ -98,7 +103,7 @@
     par[chan, 1:2, :] = jnp.concatenate([rate_ref[...]] * repeats, axis=1)
 
     pl.semaphore_wait(barrier, chan_n - 1 + ctx_n - 1)
-    par_copies = exchange(par, "chan", chan, chan_n, par_send, par_recv)
+    exchange(par, "chan", chan, chan_n, par_send, par_recv)
 
     loads[2].wait()
     loads[3].wait()
@@ -121,8 +126,8 @@
         moved = pltpu.roll(corr_ref[pl.ds(i, channels, stride=8), :], LANES - i, axis=1)
         corr += jnp.where(lane8 < LANES - i, moved, 0.0)
 
-    for copy in par_copies:
-        copy.wait_recv()
+    others = par.at[pl.ds(0, chan_n - 1)]
+    pltpu.make_async_copy(others, others, par_recv).wait()
 
     res8, rate8 = par[:, 0, :], par[:, 1, :]
     own = iota((chan_n, LANES), 1) // modes == iota((chan_n, LANES), 0)
@@ -241,6 +246,8 @@
     span_fades = scan_fades(rate, count, span)
 
     everyone = stats.at[pl.ds(0, count - 1)]
+    pltpu.make_async_copy(everyone, everyone, stats_send).wait()
+    pltpu.make_async_copy(others, others, par_send).wait()
     pltpu.make_async_copy(everyone, everyone, stats_recv).wait()
     states, mine = stats[:, 0, :], stats[:, 1, :]
     enter = total_over(rows_f[...] * states)
@@ -258,10 +265,6 @@
     tilted = shifted(sums, 4) + total_over(xd * h + x * hd)
     final = jnp.concatenate([root * plain, amp * (0.5 * plain - rate * tilted)], axis=0)
     small_ref[...] = pltpu.roll(final, lax.rem(LANES - modes * chan, LANES), axis=1)
-
-    pltpu.make_async_copy(everyone, everyone, stats_send).wait()
-    for copy in par_copies:
-        copy.wait_send()
 
 
 def solution(mesh):
@@ -293,8 +296,8 @@
                 pltpu.VMEM((1, modes), F32),
                 pltpu.VMEM((1, modes), F32),
                 pltpu.SemaphoreType.DMA((4,)),
-                pltpu.SemaphoreType.DMA((chan_n,)),
-                pltpu.SemaphoreType.DMA((chan_n,)),
+                pltpu.SemaphoreType.DMA,
+                pltpu.SemaphoreType.DMA,
                 pltpu.SemaphoreType.DMA,
                 pltpu.SemaphoreType.DMA,
             ],

time: 19.9 us -> 19.7 us (0.990)
  Pallas kernels: 18 us -> 17.8 us
where the time goes in v5:
time: 19.7 us; the launch traced here: 19.6 us
  Pallas kernels  17.8 us (90%)
  local copies, waits for them, and re-layouts  1.15 us (6%)
  between operations  0.64 us (3%)
    pallas_call x1, Pallas kernels, on_device(): pl.pallas_call(functools.partial(kernel, ctx_n, chan_n), out_shape=(jax.S...  17.8 us
    unnamed x1, local copies, waits for them, and re-layouts  0.63 us
    slice x1, local copies, waits for them, and re-layouts, on_device(): return (y, small[0:1, :modes], small[1:2, :modes])  0.52 us

profile of v5, /device:TPU:1, one launch (start us, length us, event | category | flops | bytes accessed | tf_op | source)
XLA Modules:
  0.0 19.6 jit_solution(13021206326371755982)
XLA Ops:
  0.6 17.8 %shard_map.67 = (bf16[8,4096]{1,0:T(8,128)(2,1)S(1)}, f32[2,128]{1,0:T(2,128)S(1)}) custom-call(bf16[8,4096]{1,0:T(8,128)(2,1)} %x_hbm.1, bf16[8,4096]{1,0:T(8,128)(2,1)} %g_hbm.1, f32[1,16]{1,0:T(1,128)} %res_hbm.1, f32[1,16]{1,0:T(1,128)} %rate_hbm.1), custom_call_target="tpu_custom_call" | custom-call | tf_op jit(solution)/shard_map/pallas_call | solution.py:280
  18.4 0.5 %fusion = (f32[1,16]{1,0:T(1,128)}, f32[1,16]{1,0:T(1,128)}) fusion(f32[2,128]{1,0:T(2,128)S(1)} %get-tuple-element.6), kind=kLoop, calls=%fused_computation | loop fusion | bytes 256 | tf_op jit(solution)/shard_map/slice | solution.py:308
  19.0 0.6 %copy.8 = bf16[8,4096]{1,0:T(8,128)(2,1)} copy(bf16[8,4096]{1,0:T(8,128)(2,1)S(1)} %get-tuple-element.12) | data formatting | bytes 131072

commit v6 on v5

--- a/solution.py
+++ b/solution.py
@@ -51,7 +51,7 @@
 def kernel(
     ctx_n, chan_n,
     x_hbm, g_hbm, res_hbm, rate_hbm, y_ref, small_ref,
-    rows_x, rows_g, rows_y, rows_f, corr_ref, par, out_stats, stats,
+    rows_x, rows_g, rows_y, rows_f, table_ref, corr_ref, par, out_stats, stats,
     x_ref, g_ref, res_ref, rate_ref, load_sem,
     par_send, par_recv, stats_send, stats_recv,
 ):
@@ -212,17 +212,13 @@
     samples = jnp.zeros((channels, LANES), F32)
     for k in range(modes):
         samples += amp8[:, k : k + 1] * jnp.exp(-rate8[:, k : k + 1] * lag)
-    out_high, out_low = split(amp * decay_x)
-    out_table = jnp.concatenate(
-        [twice(out_high), jnp.concatenate([out_low, jnp.zeros_like(out_low)], axis=1)], axis=0
-    )
+    out_high, out_low = split((amp * decay_x).T)
+    table_ref[:LANES, :] = jnp.concatenate([out_high, out_low], axis=1)
+    table_ref[LANES:, :] = jnp.concatenate([out_high, jnp.zeros_like(out_low)], axis=1)
 
     def expand(states):
-        outer = lax.dot_general(
-            jnp.concatenate(split(states), axis=1),
-            out_table,
-            (((1,), (1,)), ((), ())),
-            preferred_element_type=F32,
+        outer = jnp.dot(
+            jnp.concatenate(split(states), axis=1), table_ref[...], preferred_element_type=F32
         )
         return outer[:, :LANES] + outer[:, LANES:]
 
@@ -287,6 +283,7 @@
                 pltpu.VMEM((count, LANES), F32),
                 pltpu.VMEM((count, LANES), F32),
                 pltpu.VMEM((ctx_n * chan_n, LANES), F32),
+                pltpu.VMEM((2 * LANES, 2 * LANES), BF16),
                 pltpu.VMEM((channels * 8, LANES), F32),
                 pltpu.VMEM((chan_n, 2, LANES), F32),
                 pltpu.VMEM((chan_n, 2, LANES), F32),

time: 19.7 us -> 19.7 us (level)
  no operation moved by 1% of the time
where the time goes in v6:
time: 19.7 us; the launch traced here: 19.6 us
  Pallas kernels  17.8 us (90%)
  local copies, waits for them, and re-layouts  1.15 us (6%)
  between operations  0.64 us (3%)
    pallas_call x1, Pallas kernels, on_device(): pl.pallas_call(functools.partial(kernel, ctx_n, chan_n), out_shape=(jax.S...  17.8 us
    unnamed x1, local copies, waits for them, and re-layouts  0.63 us
    slice x1, local copies, waits for them, and re-layouts, on_device(): return (y, small[0:1, :modes], small[1:2, :modes])  0.52 us

profile of v6, /device:TPU:1, one launch (start us, length us, event | category | flops | bytes accessed | tf_op | source)
XLA Modules:
  0.0 19.6 jit_solution(9427091682995486128)
XLA Ops:
  0.6 17.8 %shard_map.67 = (bf16[8,4096]{1,0:T(8,128)(2,1)S(1)}, f32[2,128]{1,0:T(2,128)S(1)}) custom-call(bf16[8,4096]{1,0:T(8,128)(2,1)} %x_hbm.1, bf16[8,4096]{1,0:T(8,128)(2,1)} %g_hbm.1, f32[1,16]{1,0:T(1,128)} %res_hbm.1, f32[1,16]{1,0:T(1,128)} %rate_hbm.1), custom_call_target="tpu_custom_call" | custom-call | tf_op jit(solution)/shard_map/pallas_call | solution.py:276
  18.4 0.5 %fusion = (f32[1,16]{1,0:T(1,128)}, f32[1,16]{1,0:T(1,128)}) fusion(f32[2,128]{1,0:T(2,128)S(1)} %get-tuple-element.6), kind=kLoop, calls=%fused_computation | loop fusion | bytes 256 | tf_op jit(solution)/shard_map/slice | solution.py:305
  19.0 0.6 %copy.8 = bf16[8,4096]{1,0:T(8,128)(2,1)} copy(bf16[8,4096]{1,0:T(8,128)(2,1)S(1)} %get-tuple-element.12) | data formatting | bytes 131072

commit v7 on v6

--- a/solution.py
+++ b/solution.py
@@ -66,13 +66,13 @@
             [(res_hbm, res_ref), (rate_hbm, rate_ref), (x_hbm, x_ref), (g_hbm, g_ref)]
         )
     ]
-    loads[0].start()
-    loads[1].start()
     barrier = pltpu.get_barrier_semaphore()
     for r in farthest_first(chan_n):
         pl.semaphore_signal(
             barrier, inc=1, device_id={"chan": lax.rem(chan + r, chan_n)}, device_id_type=MESH
         )
+    loads[0].start()
+    loads[1].start()
     for r in range(1, ctx_n):
         pl.semaphore_signal(
             barrier, inc=1, device_id={"ctx": lax.rem(ctx + r, ctx_n)}, device_id_type=MESH

time: 19.7 us -> 19.7 us (level)
  no operation moved by 1% of the time
where the time goes in v7:
time: 19.7 us; the launch traced here: 19.6 us
  Pallas kernels  17.8 us (90%)
  local copies, waits for them, and re-layouts  1.15 us (6%)
  between operations  0.64 us (3%)
    pallas_call x1, Pallas kernels, on_device(): pl.pallas_call(functools.partial(kernel, ctx_n, chan_n), out_shape=(jax.S...  17.8 us
    unnamed x1, local copies, waits for them, and re-layouts  0.63 us
    slice x1, local copies, waits for them, and re-layouts, on_device(): return (y, small[0:1, :modes], small[1:2, :modes])  0.52 us

profile of v7, /device:TPU:1, one launch (start us, length us, event | category | flops | bytes accessed | tf_op | source)
XLA Modules:
  0.0 19.6 jit_solution(17848298127394551172)
XLA Ops:
  0.6 17.8 %shard_map.67 = (bf16[8,4096]{1,0:T(8,128)(2,1)S(1)}, f32[2,128]{1,0:T(2,128)S(1)}) custom-call(bf16[8,4096]{1,0:T(8,128)(2,1)} %x_hbm.1, bf16[8,4096]{1,0:T(8,128)(2,1)} %g_hbm.1, f32[1,16]{1,0:T(1,128)} %res_hbm.1, f32[1,16]{1,0:T(1,128)} %rate_hbm.1), custom_call_target="tpu_custom_call" | custom-call | tf_op jit(solution)/shard_map/pallas_call | solution.py:276
  18.4 0.5 %fusion = (f32[1,16]{1,0:T(1,128)}, f32[1,16]{1,0:T(1,128)}) fusion(f32[2,128]{1,0:T(2,128)S(1)} %get-tuple-element.6), kind=kLoop, calls=%fused_computation | loop fusion | bytes 256 | tf_op jit(solution)/shard_map/slice | solution.py:305
  19.0 0.6 %copy.8 = bf16[8,4096]{1,0:T(8,128)(2,1)} copy(bf16[8,4096]{1,0:T(8,128)(2,1)S(1)} %get-tuple-element.12) | data formatting | bytes 131072

commit v8 on v5

--- a/solution.py
+++ b/solution.py
@@ -192,18 +192,24 @@
     count = ctx_n * chan_n
     me = ctx * chan_n + chan
 
-    @pl.loop(0, count - 1)
-    def _(i):
-        to = i + jnp.where(i >= me, 1, 0)
-        to_chan = lax.rem(to, chan_n)
+    def send(line, to_chan):
         pltpu.make_async_remote_copy(
             src_ref=out_stats.at[to_chan],
             dst_ref=stats.at[me],
             send_sem=stats_send,
             recv_sem=stats_recv,
-            device_id={"ctx": lax.div(to, chan_n), "chan": to_chan},
+            device_id={"ctx": line, "chan": to_chan},
             device_id_type=MESH,
         ).start()
+
+    @pl.loop(0, ctx_n - 1)
+    def _(i):
+        line = i + jnp.where(i >= ctx, 1, 0)
+        for c in range(chan_n):
+            send(line, c)
+
+    for r in farthest_first(chan_n):
+        send(ctx, lax.rem(chan + r, chan_n))
 
     stats[me] = out_stats[chan]
 

time: 19.7 us -> 19.7 us (level)
  no operation moved by 1% of the time
where the time goes in v8:
time: 19.7 us; the launch traced here: 19.6 us
  Pallas kernels  17.8 us (90%)
  local copies, waits for them, and re-layouts  1.15 us (6%)
  between operations  0.64 us (3%)
    pallas_call x1, Pallas kernels, on_device(): pl.pallas_call(functools.partial(kernel, ctx_n, chan_n), out_shape=(jax.S...  17.8 us
    unnamed x1, local copies, waits for them, and re-layouts  0.63 us
    slice x1, local copies, waits for them, and re-layouts, on_device(): return (y, small[0:1, :modes], small[1:2, :modes])  0.52 us

profile of v8, /device:TPU:1, one launch (start us, length us, event | category | flops | bytes accessed | tf_op | source)
XLA Modules:
  0.0 19.6 jit_solution(2512333828532050238)
XLA Ops:
  0.6 17.8 %shard_map.67 = (bf16[8,4096]{1,0:T(8,128)(2,1)S(1)}, f32[2,128]{1,0:T(2,128)S(1)}) custom-call(bf16[8,4096]{1,0:T(8,128)(2,1)} %x_hbm.1, bf16[8,4096]{1,0:T(8,128)(2,1)} %g_hbm.1, f32[1,16]{1,0:T(1,128)} %res_hbm.1, f32[1,16]{1,0:T(1,128)} %rate_hbm.1), custom_call_target="tpu_custom_call" | custom-call | tf_op jit(solution)/shard_map/pallas_call | solution.py:286
  18.4 0.5 %fusion = (f32[1,16]{1,0:T(1,128)}, f32[1,16]{1,0:T(1,128)}) fusion(f32[2,128]{1,0:T(2,128)S(1)} %get-tuple-element.6), kind=kLoop, calls=%fused_computation | loop fusion | bytes 256 | tf_op jit(solution)/shard_map/slice | solution.py:314
  19.0 0.6 %copy.8 = bf16[8,4096]{1,0:T(8,128)(2,1)} copy(bf16[8,4096]{1,0:T(8,128)(2,1)S(1)} %get-tuple-element.12) | data formatting | bytes 131072
